TPU v7x, 512 devices: a whole 4x4x16 slice. The times are simulated.
512 devices in a mesh: pipe: 4 (over z_hi), dp: 16 (over y, x), tensor: 8 (over z_lo, core).
Axes of the slice: x: 4, y: 4, z: 16 (z_hi: 4, z_lo: 4; z = z_hi * 4 + z_lo), core: 2. Of those that a mesh axis runs over, the one named last changes fastest.
Arguments:
- x_in: bfloat16 [4, 2, 16, 128, 1600], P('pipe', None, 'dp', 'tensor'), may hold values from -6 to 6
- out_grad: bfloat16 [2, 16, 128, 1600], P(None, 'dp'), may hold values from -6 to 6
- layer_scale: float32 [4, 1600], P('pipe'), may hold values from 0.05 to 1
- norm_gain: float32 [4, 1600], P('pipe'), may hold values from 0.5 to 1.5
- master: float32 [4, 1600, 8192], P('pipe', 'dp', 'tensor'), may hold values from -0.15625 to 0.15625
- moment_one: float32 [4, 1600, 8192], P('pipe', 'dp', 'tensor'), may hold values from -4 to 4
- moment_two: float32 [4, 1600, 8192], P('pipe', 'dp', 'tensor'), may hold values from 0.05 to 5
Outputs:
- input_grads: bfloat16 [4, 2, 16, 128, 1600], P('pipe', None, 'dp', 'tensor')
- new_master: float32 [4, 1600, 8192], P('pipe', 'dp', 'tensor')
- new_moment_one: float32 [4, 1600, 8192], P('pipe', 'dp', 'tensor')
- new_moment_two: float32 [4, 1600, 8192], P('pipe', 'dp', 'tensor')
- scale_grads: float32 [4, 2, 1600], P('pipe')
All inputs are finite; a program needn't handle non-finite values.
Results may differ from a plain program's by a relative error of at most 0.027.
Values may be sent and summed in bfloat16 or wider, within the bound.
A program may use at most 128 MiB of HBM per device.

v0:
```python
import math
import jax
import jax.numpy as jnp
from jax import lax
from jax.sharding import PartitionSpec as P

HD = 128
beta_one = 0.9
beta_two = 0.95
adam_eps = 1e-08
learn_rate = 0.001
weight_decay = 0.05
adam_step = 100.0
norm_eps = 1e-06


def from_behind(block, axis, distance):
    devices = range(lax.axis_size(axis))
    route = [(i - distance, i) for i in devices if i - distance in devices]
    return lax.ppermute(block, axis, route)


def normalize(values_in):
    inverse = lax.rsqrt(jnp.mean(values_in * values_in, axis=-1, keepdims=True) + norm_eps)
    return (inverse, values_in * inverse)


def select_micro(array, micro_index):
    return lax.dynamic_index_in_dim(array, micro_index, 0, keepdims=False)


def store_slot(buffer, value, slot_index):
    return lax.dynamic_update_index_in_dim(buffer, value, slot_index, 0)


def local(x_in, out_grad, layer_scale, norm_gain, master, moment_one, moment_two):
    n_pipe = lax.axis_size("pipe")
    n_tensor = lax.axis_size("tensor")
    pipe_rank = lax.axis_index("pipe")
    micro_count = x_in.shape[1]
    images = x_in.shape[2]
    shard_len = x_in.shape[3]
    channels = x_in.shape[4]
    seq_len = shard_len * n_tensor
    row_start = lax.axis_index("tensor") * shard_len
    head_cols = master.shape[2] // 4
    local_heads = head_cols // HD
    score_root = math.sqrt(HD)
    scale_vec = layer_scale[0]
    gain_vec = norm_gain[0]
    weights = lax.all_gather(master[0].astype(jnp.bfloat16), "dp", axis=0, tiled=True)
    w_qkv = weights[:, : 3 * head_cols]
    w_out = weights[:, 3 * head_cols :]
    full_x = lax.all_gather(x_in[0], "tensor", axis=2, tiled=True).astype(jnp.float32)
    full_inverse, full_unit = normalize(full_x)
    normed = (full_unit * gain_vec).astype(jnp.bfloat16)
    local_unit = lax.dynamic_slice_in_dim(full_unit, row_start, shard_len, 2)
    projected = jnp.einsum(
        "mbsd,dc->mbsc", normed, w_qkv, preferred_element_type=jnp.float32
    ).astype(jnp.bfloat16)
    projected = projected.reshape(micro_count, images, seq_len, 3, local_heads, HD)
    query = projected[:, :, :, 0]
    keys = projected[:, :, :, 1]
    values = projected[:, :, :, 2]
    scores = (
        jnp.einsum("mbqhe,mbkhe->mbhqk", query, keys, preferred_element_type=jnp.float32)
        / score_root
    )
    probs = jax.nn.softmax(scores, axis=-1)
    probs_low = probs.astype(jnp.bfloat16)
    attended = jnp.einsum(
        "mbhqk,mbkhe->mbqhe", probs_low, values, preferred_element_type=jnp.float32
    ).astype(jnp.bfloat16)
    attended_flat = attended.reshape(micro_count, images, seq_len, head_cols)

    def backward_segment(micro_index, incoming):
        query_now = select_micro(query, micro_index)
        keys_now = select_micro(keys, micro_index)
        values_now = select_micro(values, micro_index)
        probs_now = select_micro(probs, micro_index)
        probs_low_now = select_micro(probs_low, micro_index)
        attended_now = select_micro(attended, micro_index)
        scaled = (scale_vec * incoming.astype(jnp.float32)).astype(jnp.bfloat16)
        d_att = jnp.einsum("bsd,dc->bsc", scaled, w_out, preferred_element_type=jnp.float32).astype(
            jnp.bfloat16
        )
        d_att = d_att.reshape(images, seq_len, local_heads, HD)
        d_prob = jnp.einsum(
            "bqhe,bkhe->bhqk", d_att, values_now, preferred_element_type=jnp.float32
        )
        row_delta = jnp.einsum(
            "bqhe,bqhe->bhq", d_att, attended_now, preferred_element_type=jnp.float32
        )
        d_score = (probs_now * (d_prob - row_delta[..., None]) / score_root).astype(jnp.bfloat16)
        d_query = jnp.einsum(
            "bhqk,bkhe->bqhe", d_score, keys_now, preferred_element_type=jnp.float32
        ).astype(jnp.bfloat16)
        d_keys = jnp.einsum(
            "bhqk,bqhe->bkhe", d_score, query_now, preferred_element_type=jnp.float32
        ).astype(jnp.bfloat16)
        d_values = jnp.einsum(
            "bhqk,bqhe->bkhe", probs_low_now, d_att, preferred_element_type=jnp.float32
        ).astype(jnp.bfloat16)
        d_proj = jnp.concatenate([d_query, d_keys, d_values], axis=2).reshape(
            images, seq_len, 3 * head_cols
        )
        partial_sum = jnp.einsum("bsc,dc->bsd", d_proj, w_qkv, preferred_element_type=jnp.float32)
        return (partial_sum, d_proj, scaled)

    def spare_segment(micro_index, incoming):
        return (
            jnp.zeros((images, seq_len, channels), jnp.float32),
            jnp.zeros((images, seq_len, 3 * head_cols), jnp.bfloat16),
            jnp.zeros((images, seq_len, channels), jnp.bfloat16),
        )

    segments = n_pipe + micro_count - 1
    is_last = pipe_rank == n_pipe - 1
    received = jnp.zeros((images, seq_len, channels), jnp.bfloat16)
    slots = micro_count + 1
    grads_out = jnp.zeros((slots, images, shard_len, channels), jnp.bfloat16)
    proj_saved = jnp.zeros((slots, images, seq_len, 3 * head_cols), jnp.bfloat16)
    scaled_saved = jnp.zeros((slots, images, seq_len, channels), jnp.bfloat16)
    grad_saved = jnp.zeros((slots, images, seq_len, channels), jnp.bfloat16)
    gain_part = jnp.zeros((channels,), jnp.float32)
    for segment_step in range(segments):
        micro_index = segment_step - (n_pipe - 1) + pipe_rank
        active = jnp.logical_and(micro_index >= 0, micro_index < micro_count)
        micro_index = jnp.clip(micro_index, 0, micro_count - 1)
        slot_index = jnp.where(active, micro_index, micro_count)
        arrived = received
        incoming = jnp.where(is_last, select_micro(out_grad, micro_index), arrived)
        partial_sum, d_proj, scaled = lax.cond(
            active, backward_segment, spare_segment, micro_index, incoming
        )
        pieces = partial_sum.astype(jnp.bfloat16).reshape(images, n_tensor, shard_len, channels)
        landed = lax.all_to_all(pieces, "tensor", split_axis=1, concat_axis=1, tiled=True)
        own_d = jnp.sum(landed.astype(jnp.float32), axis=1)
        d_normed = lax.all_gather(own_d.astype(jnp.bfloat16), "tensor", axis=1, tiled=True).astype(
            own_d.dtype
        )
        own_unit = select_micro(local_unit, micro_index)
        sel_unit = select_micro(full_unit, micro_index)
        sel_inverse = select_micro(full_inverse, micro_index)
        d_unit = d_normed * gain_vec
        d_input = sel_inverse * (
            d_unit - sel_unit * jnp.mean(d_unit * sel_unit, axis=-1, keepdims=True)
        )
        passed = (incoming.astype(jnp.float32) + d_input).astype(jnp.bfloat16)
        own_passed = lax.dynamic_slice_in_dim(passed, row_start, shard_len, 1)
        gain_part = gain_part + jnp.where(active, jnp.sum(own_d * own_unit, axis=(0, 1)), 0.0)
        grads_out = store_slot(grads_out, own_passed, slot_index)
        proj_saved = store_slot(proj_saved, d_proj, slot_index)
        scaled_saved = store_slot(scaled_saved, scaled, slot_index)
        grad_saved = store_slot(grad_saved, incoming, slot_index)
        if segment_step + 1 < segments:
            received = from_behind(passed, "pipe", -1)
    grads_kept = grads_out[:micro_count]
    proj_kept = proj_saved[:micro_count]
    scaled_kept = scaled_saved[:micro_count]
    grad_kept = grad_saved[:micro_count]
    grad_qkv = jnp.einsum("mbsd,mbsc->dc", normed, proj_kept, preferred_element_type=jnp.float32)
    grad_out = jnp.einsum(
        "mbsd,mbsc->dc", scaled_kept, attended_flat, preferred_element_type=jnp.float32
    )
    weight_grad = lax.psum_scatter(
        jnp.concatenate([grad_qkv, grad_out], axis=1).astype(jnp.bfloat16),
        "dp",
        scatter_dimension=0,
        tiled=True,
    ).astype(jnp.float32)
    summed_out = jnp.einsum(
        "mbsd,mbsc->dc", grad_kept, attended_flat, preferred_element_type=jnp.float32
    )
    scale_part = jnp.sum(w_out.astype(jnp.float32) * summed_out, axis=1)
    scale_grad, gain_grad = lax.psum((scale_part, gain_part), ("dp", "tensor"))
    bias_one = 1.0 - beta_one**adam_step
    bias_two = 1.0 - beta_two**adam_step
    first_new = beta_one * moment_one[0] + (1.0 - beta_one) * weight_grad
    second_new = beta_two * moment_two[0] + (1.0 - beta_two) * weight_grad * weight_grad
    update = first_new / bias_one / (jnp.sqrt(second_new / bias_two) + adam_eps)
    master_new = master[0] - learn_rate * (update + weight_decay * master[0])
    scale_both = jnp.stack([scale_grad, gain_grad])
    return (grads_kept[None], master_new[None], first_new[None], second_new[None], scale_both[None])


def solution(mesh):
    placed = (
        P("pipe", None, "dp", "tensor", None),
        P(None, "dp", None, None),
        P("pipe", None),
        P("pipe", None),
        P("pipe", "dp", "tensor"),
        P("pipe", "dp", "tensor"),
        P("pipe", "dp", "tensor"),
    )
    return jax.shard_map(
        local,
        mesh=mesh,
        in_specs=placed,
        out_specs=(
            P("pipe", None, "dp", "tensor", None),
            P("pipe", "dp", "tensor"),
            P("pipe", "dp", "tensor"),
            P("pipe", "dp", "tensor"),
            P("pipe", None, None),
        ),
        check_vma=False,
    )
```

profile of v0, /device:TPU:128, one launch (start us, length us, event | category | flops | bytes accessed | tf_op | source)
XLA Modules:
  0.0 1397.1 jit_solution(9497189529222593364)
XLA Ops:
  9.8 17.2 %all-gather = bf16[1,2,1,128,1600]{4,3,2,1,0:T(8,128)(2,1)S(1)} all-gather(bf16[1,2,1,16,1600]{4,3,2,1,0:T(8,128)(2,1)} %param.17), channel_id=2, replica_groups=mesh['pipe'=4,'dp'=16,'tensor'=8] {'tensor'}, dimensions={3}, use_global_device_ids=true | all-gather | bytes 921600 | tf_op jit(solution)/shard_map/all_gather | solution.py:54
  28.1 50.7 %all-gather.9.cloned.1.call-done = bf16[16,100,1024]{2,1,0:T(8,128)(2,1)} async-done(((bf16[1,100,1024]{2,1,0:T(8,128)(2,1)}), bf16[16,100,1024]{2,1,0:T(8,128)(2,1)}) %all-gather.9.cloned.1.call-update) | async-done | bytes 3276816 | tf_op jit(solution)/shard_map/all_gather | solution.py:51
  78.8 2.9 reshape.819
  81.7 3.4 fusion.113
  96.1 2.1 convolution_convert_fusion.20
  98.2 2.3 conditional.5
  102.5 4.8 all-to-all-start
  108.7 2.3 constant_dynamic-slice_fusion
  111.4 2.4 copy.217
  115.1 5.5 all-to-all-done
  122.4 15.6 %all-gather.1 = bf16[128,1600]{1,0:T(8,128)(2,1)} all-gather(bf16[16,1600]{1,0:T(8,128)(2,1)S(1)} %convert_element_type.421), channel_id=3, replica_groups=mesh['pipe'=4,'dp'=16,'tensor'=8] {'tensor'}, dimensions={0}, use_global_device_ids=true | all-gather | bytes 460800 | tf_op jit(solution)/shard_map/all_gather | solution.py:139
  141.5 2.2 fusion.145
  143.8 2.1 collective-permute-start
  147.2 39.6 %collective-permute-done = bf16[1,128,1600]{1,2,0:T(8,128)(2,1)} collective-permute-done((bf16[1,128,1600]{1,2,0:T(8,128)(2,1)}, bf16[1,128,1600]{1,2,0:T(8,128)(2,1)}, u32[]{:S(2)}, u32[]{:S(2)}) %collective-permute-start) | collective-permute-done | bytes 409632 | tf_op jit(solution)/shard_map/ppermute | solution.py:20
  189.9 2.7 conditional.6
  194.6 4.1 all-to-all-start.1
  198.7 2.4 copy.231
  201.1 10.9 all-to-all-done.1
  213.7 15.6 %all-gather.2 = bf16[128,1600]{1,0:T(8,128)(2,1)} all-gather(bf16[16,1600]{1,0:T(8,128)(2,1)S(1)} %convert_element_type.429), channel_id=4, replica_groups=mesh['pipe'=4,'dp'=16,'tensor'=8] {'tensor'}, dimensions={0}, use_global_device_ids=true | all-gather | bytes 460800 | tf_op jit(solution)/shard_map/all_gather | solution.py:139
  229.2 2.0 copy.230
  232.9 2.2 fusion.139
  235.1 2.2 collective-permute-start.1
  237.3 98.2 %collective-permute-done.1 = bf16[1,128,1600]{1,2,0:T(8,128)(2,1)} collective-permute-done((bf16[1,128,1600]{1,2,0:T(8,128)(2,1)}, bf16[1,128,1600]{1,2,0:T(8,128)(2,1)}, u32[]{:S(2)}, u32[]{:S(2)}) %collective-permute-start.1) | collective-permute-done | bytes 409632 | tf_op jit(solution)/shard_map/ppermute | solution.py:20
  335.5 2.1 bitcast_dynamic-update-slice_fusion.1
  337.7 34.1 %conditional.7 = (bf16[1,128,1600]{1,2,0:T(8,128)(2,1)}, bf16[1,1,128,768]{3,2,0,1:T(8,128)(2,1)}, bf16[1,1,128,1600]{2,3,0,1:T(8,128)(2,1)}) conditional(s32[]{:T(128)} %convert_element_type.434, () %tuple.72, (s32[]{:T(128)}, bf16[2,1,128,2,128]{4,2,3,0,1:T(8,128)(2,1)}, f32[2,1,2,128,128]{3,4,2,0,1:T(8,128)S(1)}, f32[1,1600]{1,0:T(1,128)S(1)}, ...), branch_computations={%region_11.12_spmd, %region_12.13_spmd} | conditional | flops 454803200 | bytes 11565162 | solution.py:133
  373.8 4.1 all-to-all-start.2
  377.9 2.3 copy.245
  380.3 2.3 copy.259
  382.6 2.4 copy.273
  399.1 16.0 %all-gather.3 = bf16[128,1600]{1,0:T(8,128)(2,1)} all-gather(bf16[16,1600]{1,0:T(8,128)(2,1)S(1)} %convert_element_type.437), channel_id=5, replica_groups=mesh['pipe'=4,'dp'=16,'tensor'=8] {'tensor'}, dimensions={0}, use_global_device_ids=true | all-gather | bytes 460800 | tf_op jit(solution)/shard_map/all_gather | solution.py:139
  425.6 38.5 %collective-permute-done.2 = bf16[1,128,1600]{1,2,0:T(8,128)(2,1)S(1)} collective-permute-done((bf16[1,128,1600]{1,2,0:T(8,128)(2,1)S(1)}, bf16[1,128,1600]{1,2,0:T(8,128)(2,1)S(1)}, u32[]{:S(2)}, u32[]{:S(2)}) %collective-permute-start.2) | collective-permute-done | bytes 409632 | tf_op jit(solution)/shard_map/ppermute | solution.py:20
  465.1 34.2 %conditional.8 = (bf16[1,128,1600]{1,2,0:T(8,128)(2,1)}, bf16[1,1,128,768]{3,2,0,1:T(8,128)(2,1)}, bf16[1,1,128,1600]{2,3,0,1:T(8,128)(2,1)}) conditional(s32[]{:T(128)} %convert_element_type.442, () %tuple.74, (s32[]{:T(128)}, bf16[2,1,128,2,128]{4,2,3,0,1:T(8,128)(2,1)}, f32[2,1,2,128,128]{3,4,2,0,1:T(8,128)S(1)}, f32[1,1600]{1,0:T(1,128)S(1)}, ...), branch_computations={%region_15.16_spmd, %region_16.17_spmd} | conditional | flops 454803200 | bytes 11565162 | solution.py:133
  499.3 2.0 copy.255
  501.3 4.1 all-to-all-start.3
  524.3 16.0 %all-gather.4 = bf16[128,1600]{1,0:T(8,128)(2,1)} all-gather(bf16[16,1600]{1,0:T(8,128)(2,1)S(1)} %convert_element_type.445), channel_id=6, replica_groups=mesh['pipe'=4,'dp'=16,'tensor'=8] {'tensor'}, dimensions={0}, use_global_device_ids=true | all-gather | bytes 460800 | tf_op jit(solution)/shard_map/all_gather | solution.py:139
  543.9 2.2 fusion.127
  546.1 2.1 collective-permute-start.3
  553.3 36.9 %collective-permute-done.3 = bf16[1,128,1600]{1,2,0:T(8,128)(2,1)} collective-permute-done((bf16[1,128,1600]{1,2,0:T(8,128)(2,1)}, bf16[1,128,1600]{1,2,0:T(8,128)(2,1)}, u32[]{:S(2)}, u32[]{:S(2)}) %collective-permute-start.3) | collective-permute-done | bytes 409632 | tf_op jit(solution)/shard_map/ppermute | solution.py:20
  590.2 2.2 bitcast_dynamic-update-slice_fusion.3
  592.4 2.3 conditional.9
  594.7 2.0 copy.269
  596.7 4.1 all-to-all-start.4
  608.2 76.2 %fusion = bf16[112,1024]{1,0:T(8,128)(2,1)} fusion(bf16[1600,1024]{1,0:T(8,128)(2,1)S(1)} %pad_maximum_fusion.5), kind=kCustom, calls=%all-reduce-scatter | all-reduce-scatter fusion | flops 1835009 | bytes 3508224
  685.4 3.7 collective-permute-start.4
  689.1 4.1 collective-permute-start.5
  693.2 2.0 fusion.112
  703.2 15.6 %all-gather.5 = bf16[128,1600]{1,0:T(8,128)(2,1)S(1)} all-gather(bf16[16,1600]{1,0:T(8,128)(2,1)S(1)} %get-tuple-element.430), channel_id=7, replica_groups=mesh['pipe'=4,'dp'=16,'tensor'=8] {'tensor'}, dimensions={0}, use_global_device_ids=true | all-gather | bytes 460800 | tf_op jit(solution)/shard_map/all_gather | solution.py:139
  721.0 668.4 %all-reduce.2 = (f32[1,1600]{1,0:T(1,128)S(1)}, f32[1,1600]{1,0:T(1,128)S(1)}) all-reduce(f32[1,1600]{1,0:T(1,128)S(1)} %stack.10, f32[1,1600]{1,0:T(1,128)S(1)} %stack.9), channel_id=1, replica_groups=mesh['pipe'=4,'dp'=16,'tensor'=8] {'dp','tensor'}, use_global_device_ids=true, to_apply=%region_31.32 | all-reduce | flops 3200 | bytes 25600 | tf_op jit(solution)/shard_map/psum | solution.py:176
  (231 shorter events, 183.1 us)
Async XLA Ops:
  7.2 20.1 %copy-start.2 = (bf16[2,1,128,1600]{2,3,1,0:T(8,128)(2,1)S(1)}, bf16[2,1,128,1600]{2,3,1,0:T(8,128)(2,1)}, u32[]{:S(2)}) copy-start(bf16[2,1,128,1600]{2,3,1,0:T(8,128)(2,1)} %param.18) | copy-start | bytes 2457604
  7.2 71.6 %all-gather.9.cloned.1.call-start = ((), (), s32[]{:S(2)}) async-start(), calls=%async_computation.5 | async-start | bytes 3620864 | tf_op jit(solution)/shard_map/all_gather | solution.py:51
  27.0 1.1 copy-start.5
  27.3 54.4 %copy-start.44 = (f32[2,128]{1,0:T(2,128)}, f32[2,128]{1,0:T(2,128)S(1)}, u32[]{:S(2)}) copy-start(f32[2,128]{1,0:T(2,128)S(1)} %add_rsqrt_fusion) | copy-start | bytes 3076
  81.7 3.5 copy-start.1
  88.3 0.8 copy-start.35
  88.3 5.4 copy-start.34
  93.7 4.5 copy-start.42
  102.5 18.2 %all-to-all-start = ((bf16[1,8,16,1600]{3,2,0,1:T(8,128)(2,1)}), bf16[1,8,16,1600]{3,2,0,1:T(8,128)(2,1)}, u32[]{:S(2)}, u32[]{:S(2)}) async-start(bf16[1,8,16,1600]{3,2,0,1:T(8,128)(2,1)} %bitcast.535), calls=%async_computation | async-start | bytes 851968 | tf_op jit(solution)/shard_map/all_to_all | solution.py:137
  108.6 2.7 copy-start
  139.9 1.6 copy-start.11
  143.8 43.1 %collective-permute-start = (bf16[1,128,1600]{1,2,0:T(8,128)(2,1)}, bf16[1,128,1600]{1,2,0:T(8,128)(2,1)}, u32[]{:S(2)}, u32[]{:S(2)}) collective-permute-start(bf16[1,128,1600]{1,2,0:T(8,128)(2,1)} %fusion.145), channel_id=1, source_target_pairs={{128,0},{256,128},{384,256},{129,1},{257,129},{385,257},{130,2},{2... | collective-permute-start | bytes 1228808 | tf_op jit(solution)/shard_map/ppermute | solution.py:20
  145.9 41.0 %copy-start.3 = (bf16[2,1,128,1600]{2,3,1,0:T(8,128)(2,1)S(1)}, bf16[2,1,128,1600]{2,3,1,0:T(8,128)(2,1)}, u32[]{:S(2)}) copy-start(bf16[2,1,128,1600]{2,3,1,0:T(8,128)(2,1)} %param.18) | copy-start | bytes 2457604
  188.8 1.1 copy-start.25
  194.6 17.4 %all-to-all-start.1 = ((bf16[1,8,16,1600]{3,2,0,1:T(8,128)(2,1)}), bf16[1,8,16,1600]{3,2,0,1:T(8,128)(2,1)}, u32[]{:S(2)}, u32[]{:S(2)}) async-start(bf16[1,8,16,1600]{3,2,0,1:T(8,128)(2,1)} %bitcast.537), calls=%async_computation.1 | async-start | bytes 851968 | tf_op jit(solution)/shard_map/all_to_all | solution.py:137
  231.2 1.6 copy-start.9
  235.1 100.4 %collective-permute-start.1 = (bf16[1,128,1600]{1,2,0:T(8,128)(2,1)}, bf16[1,128,1600]{1,2,0:T(8,128)(2,1)}, u32[]{:S(2)}, u32[]{:S(2)}) collective-permute-start(bf16[1,128,1600]{1,2,0:T(8,128)(2,1)} %fusion.139), channel_id=1, source_target_pairs={{128,0},{256,128},{384,256},{129,1},{257,129},{385,257},{130,2},{2... | collective-permute-start | bytes 1228808 | tf_op jit(solution)/shard_map/ppermute | solution.py:20
  364.7 1.6 copy-start.20
  373.8 23.6 %all-to-all-start.2 = ((bf16[1,8,16,1600]{3,2,0,1:T(8,128)(2,1)}), bf16[1,8,16,1600]{3,2,0,1:T(8,128)(2,1)}, u32[]{:S(2)}, u32[]{:S(2)}) async-start(bf16[1,8,16,1600]{3,2,0,1:T(8,128)(2,1)} %bitcast.534), calls=%async_computation.2 | async-start | bytes 851968 | tf_op jit(solution)/shard_map/all_to_all | solution.py:137
  398.4 0.7 copy-start.30
  417.0 1.6 copy-start.8
  417.0 5.1 copy-start.41
  418.6 45.4 %copy-start.4 = (bf16[2,1,128,1600]{2,3,1,0:T(8,128)(2,1)S(1)}, bf16[2,1,128,1600]{2,3,1,0:T(8,128)(2,1)}, u32[]{:S(2)}) copy-start(bf16[2,1,128,1600]{2,3,1,0:T(8,128)(2,1)} %param.18) | copy-start | bytes 2457604
  420.1 45.0 %copy-start.22 = (bf16[1,128,1600]{1,2,0:T(8,128)(2,1)}, bf16[1,128,1600]{1,2,0:T(8,128)(2,1)S(1)}, u32[]{:S(2)}) copy-start(bf16[1,128,1600]{1,2,0:T(8,128)(2,1)S(1)} %fusion.133) | copy-start | bytes 1228804
  420.1 43.9 %collective-permute-start.2 = (bf16[1,128,1600]{1,2,0:T(8,128)(2,1)S(1)}, bf16[1,128,1600]{1,2,0:T(8,128)(2,1)S(1)}, u32[]{:S(2)}, u32[]{:S(2)}) collective-permute-start(bf16[1,128,1600]{1,2,0:T(8,128)(2,1)S(1)} %fusion.133), channel_id=1, source_target_pairs={{128,0},{256,128},{384,256},{129,1},{257,129},{385,257},{130,2},{2... | collective-permute-start | bytes 1228808 | tf_op jit(solution)/shard_map/ppermute | solution.py:20
  422.1 43.0 %copy-start.36 = (bf16[3,1,16,1600]{3,2,0,1:T(8,128)(2,1)}, bf16[3,1,16,1600]{3,2,0,1:T(8,128)(2,1)S(1)}, u32[]{:S(2)}) copy-start(bf16[3,1,16,1600]{3,2,0,1:T(8,128)(2,1)S(1)} %constant_dynamic-update-slice_fusion.14) | copy-start | bytes 460804
  492.2 1.6 copy-start.21
  501.3 21.3 %all-to-all-start.3 = ((bf16[1,8,16,1600]{3,2,0,1:T(8,128)(2,1)}), bf16[1,8,16,1600]{3,2,0,1:T(8,128)(2,1)}, u32[]{:S(2)}, u32[]{:S(2)}) async-start(bf16[1,8,16,1600]{3,2,0,1:T(8,128)(2,1)} %bitcast.536), calls=%async_computation.3 | async-start | bytes 851968 | tf_op jit(solution)/shard_map/all_to_all | solution.py:137
  542.3 1.6 copy-start.7
  546.1 44.2 %collective-permute-start.3 = (bf16[1,128,1600]{1,2,0:T(8,128)(2,1)}, bf16[1,128,1600]{1,2,0:T(8,128)(2,1)}, u32[]{:S(2)}, u32[]{:S(2)}) collective-permute-start(bf16[1,128,1600]{1,2,0:T(8,128)(2,1)} %fusion.127), channel_id=1, source_target_pairs={{128,0},{256,128},{384,256},{129,1},{257,129},{385,257},{130,2},{2... | collective-permute-start | bytes 1228808 | tf_op jit(solution)/shard_map/ppermute | solution.py:20
  594.7 7.8 copy-start.6
  594.7 7.8 copy-start.45
  596.7 103.9 %all-to-all-start.4 = ((bf16[1,8,16,1600]{3,2,0,1:T(8,128)(2,1)}), bf16[1,8,16,1600]{3,2,0,1:T(8,128)(2,1)}, u32[]{:S(2)}, u32[]{:S(2)}) async-start(bf16[1,8,16,1600]{3,2,0,1:T(8,128)(2,1)} %bitcast.151), calls=%async_computation.4 | async-start | bytes 851968 | tf_op jit(solution)/shard_map/all_to_all | solution.py:137
  602.5 3.8 copy-start.12
  684.4 11.5 copy-start.24
  685.4 10.5 collective-permute-start.4
  689.1 6.8 collective-permute-start.5
  693.2 3.4 copy-start.23
  693.2 3.4 copy-start.38
  693.2 3.4 copy-start.39
  697.1 4.7 copy-start.27
  697.1 4.7 copy-start.29
  697.1 4.7 copy-start.31
  697.1 4.7 copy-start.33
  700.6 18.5 %copy-start.10 = (f32[1,1,128,1600]{2,3,1,0:T(8,128)S(1)}, f32[1,1,128,1600]{2,3,1,0:T(8,128)}, u32[]{:S(2)}) copy-start(f32[1,1,128,1600]{2,3,1,0:T(8,128)} %copy.273) | copy-start | bytes 2457604
  703.2 16.3 %copy-start.17 = (bf16[1,128,1600]{1,2,0:T(8,128)(2,1)S(1)}, bf16[1,128,1600]{1,2,0:T(8,128)(2,1)}, u32[]{:S(2)}) copy-start(bf16[1,128,1600]{1,2,0:T(8,128)(2,1)} %get-tuple-element.408) | copy-start | bytes 1228804
  703.2 16.3 %copy-start.46 = (f32[16]{0:T(128)S(1)}, f32[16]{0:T(128)}, u32[]{:S(2)}) copy-start(f32[16]{0:T(128)} %dynamic-slice.8) | copy-start | bytes 196
  719.4 0.9 copy-start.37
  (3 other events, 1.9 us)
Sparse Core Ops, SparseCore 0:
  11.6 67.1 all-gather.8
where the time goes:
time: 1410 us; the launch traced here: 1400 us
  blocking collectives  840 us (60%)
  waiting for transfers between devices  281 us (20%)
  local copies, waits for them, and re-layouts  143 us (10%)
  other arithmetic  47.2 us (3%)
  starting transfers between devices  37.3 us (3%)
  matrix products  31.9 us (2%)
  between operations  15.6 us (1%)
    psum x1, blocking collectives, local(): scale_grad, gain_grad = lax.psum((scale_part, gain_part), ('dp', 'tensor'))  668 us
    ppermute x4, waiting for transfers between devices, from_behind(): return lax.ppermute(block, axis, route)  213 us
    all_gather x5, blocking collectives, local(): lax.all_gather(own_d.astype(jnp.bfloat16), 'tensor', axis=1, tiled=True)  78.7 us
    unnamed x1, blocking collectives  76.2 us
    all_gather x1, waiting for transfers between devices, local(): lax.all_gather(master[0].astype(jnp.bfloat16), 'dp', axis=0, tiled=True)  50.7 us
    another operation x23, local copies, waits for them, and re-layouts  32.1 us
  transfers between devices with their start and end apart: 12, of which 8 were waited for; matrix products, arithmetic and copies ran while one was open for 11% of the time, Pallas kernels for 0%

commit v1 on v0

--- a/solution.py
+++ b/solution.py
@@ -173,7 +173,7 @@
         "mbsd,mbsc->dc", grad_kept, attended_flat, preferred_element_type=jnp.float32
     )
     scale_part = jnp.sum(w_out.astype(jnp.float32) * summed_out, axis=1)
-    scale_grad, gain_grad = lax.psum((scale_part, gain_part), ("dp", "tensor"))
+    scale_grad, gain_grad = lax.psum(lax.psum((scale_part, gain_part), "tensor"), "dp")
     bias_one = 1.0 - beta_one**adam_step
     bias_two = 1.0 - beta_two**adam_step
     first_new = beta_one * moment_one[0] + (1.0 - beta_one) * weight_grad

time: 1410 us -> 841 us (0.60)
  blocking collectives: 840 us -> 273 us
    psum x1 -> x2, blocking collectives: 668 us -> 101 us  [the longest x1 71.7 us: local(): lax.psum(lax.psum((scale_part, gain_part), 'tensor'), 'dp')]
  transfers between devices with their start and end apart: 12 -> 12, of which waited for: 8 -> 8; matrix products, arithmetic and copies ran while one was open for 11% -> 18% of each run, Pallas kernels for 0% -> 0%
where the time goes in v1:
time: 841 us; the launch traced here: 829 us
  waiting for transfers between devices  281 us (33%)
  blocking collectives  273 us (32%)
  local copies, waits for them, and re-layouts  143 us (17%)
  other arithmetic  47.2 us (6%)
  starting transfers between devices  37.3 us (4%)
  matrix products  31.9 us (4%)
  between operations  15.6 us (2%)
    ppermute x4, waiting for transfers between devices, from_behind(): return lax.ppermute(block, axis, route)  213 us
    all_gather x5, blocking collectives, local(): lax.all_gather(own_d.astype(jnp.bfloat16), 'tensor', axis=1, tiled=True)  78.7 us
    unnamed x1, blocking collectives  76.2 us
    psum x1, blocking collectives, local(): lax.psum(lax.psum((scale_part, gain_part), 'tensor'), 'dp')  71.7 us
    all_gather x1, waiting for transfers between devices, local(): lax.all_gather(master[0].astype(jnp.bfloat16), 'dp', axis=0, tiled=True)  50.7 us
    another operation x23, local copies, waits for them, and re-layouts  32.1 us
    psum x1, blocking collectives, local(): lax.psum((scale_part, gain_part), 'tensor')  28.9 us
    dynamic_update_slice x15, local copies, waits for them, and re-layouts, store_slot(): return lax.dynamic_update_index_in_dim(buffer, value, slot_index, 0)  21.4 us
  transfers between devices with their start and end apart: 12, of which 8 were waited for; matrix products, arithmetic and copies ran while one was open for 18% of the time, Pallas kernels for 0%

profile of v1, /device:TPU:128, one launch (start us, length us, event | category | flops | bytes accessed | tf_op | source)
XLA Modules:
  0.0 829.3 jit_solution(11837085025680797687)
XLA Ops:
  9.8 17.2 %all-gather = bf16[1,2,1,128,1600]{4,3,2,1,0:T(8,128)(2,1)S(1)} all-gather(bf16[1,2,1,16,1600]{4,3,2,1,0:T(8,128)(2,1)} %param.17), channel_id=2, replica_groups=mesh['pipe'=4,'dp'=16,'tensor'=8] {'tensor'}, dimensions={3}, use_global_device_ids=true | all-gather | bytes 921600 | tf_op jit(solution)/shard_map/all_gather | solution.py:54
  28.1 50.7 %all-gather.9.cloned.1.call-done = bf16[16,100,1024]{2,1,0:T(8,128)(2,1)} async-done(((bf16[1,100,1024]{2,1,0:T(8,128)(2,1)}), bf16[16,100,1024]{2,1,0:T(8,128)(2,1)}) %all-gather.9.cloned.1.call-update) | async-done | bytes 3276816 | tf_op jit(solution)/shard_map/all_gather | solution.py:51
  78.8 2.9 reshape.819
  81.7 3.4 fusion.113
  96.1 2.1 convolution_convert_fusion.20
  98.2 2.3 conditional.5
  102.5 4.8 all-to-all-start
  108.7 2.3 constant_dynamic-slice_fusion
  111.4 2.4 copy.217
  115.1 5.5 all-to-all-done
  122.4 15.6 %all-gather.1 = bf16[128,1600]{1,0:T(8,128)(2,1)} all-gather(bf16[16,1600]{1,0:T(8,128)(2,1)S(1)} %convert_element_type.421), channel_id=3, replica_groups=mesh['pipe'=4,'dp'=16,'tensor'=8] {'tensor'}, dimensions={0}, use_global_device_ids=true | all-gather | bytes 460800 | tf_op jit(solution)/shard_map/all_gather | solution.py:139
  141.5 2.2 fusion.145
  143.8 2.1 collective-permute-start
  147.2 39.6 %collective-permute-done = bf16[1,128,1600]{1,2,0:T(8,128)(2,1)} collective-permute-done((bf16[1,128,1600]{1,2,0:T(8,128)(2,1)}, bf16[1,128,1600]{1,2,0:T(8,128)(2,1)}, u32[]{:S(2)}, u32[]{:S(2)}) %collective-permute-start) | collective-permute-done | bytes 409632 | tf_op jit(solution)/shard_map/ppermute | solution.py:20
  189.9 2.7 conditional.6
  194.6 4.1 all-to-all-start.1
  198.7 2.4 copy.231
  201.1 10.9 %all-to-all-done.1 = bf16[1,8,16,1600]{3,2,0,1:T(8,128)(2,1)} async-done(((bf16[1,8,16,1600]{3,2,0,1:T(8,128)(2,1)}), bf16[1,8,16,1600]{3,2,0,1:T(8,128)(2,1)}, u32[]{:S(2)}, u32[]{:S(2)}) %all-to-all-start.1) | async-done | bytes 409632 | tf_op jit(solution)/shard_map/all_to_all | solution.py:137
  213.7 15.6 %all-gather.2 = bf16[128,1600]{1,0:T(8,128)(2,1)} all-gather(bf16[16,1600]{1,0:T(8,128)(2,1)S(1)} %convert_element_type.429), channel_id=4, replica_groups=mesh['pipe'=4,'dp'=16,'tensor'=8] {'tensor'}, dimensions={0}, use_global_device_ids=true | all-gather | bytes 460800 | tf_op jit(solution)/shard_map/all_gather | solution.py:139
  229.2 2.0 copy.230
  232.9 2.2 fusion.139
  235.1 2.2 collective-permute-start.1
  237.3 98.2 %collective-permute-done.1 = bf16[1,128,1600]{1,2,0:T(8,128)(2,1)} collective-permute-done((bf16[1,128,1600]{1,2,0:T(8,128)(2,1)}, bf16[1,128,1600]{1,2,0:T(8,128)(2,1)}, u32[]{:S(2)}, u32[]{:S(2)}) %collective-permute-start.1) | collective-permute-done | bytes 409632 | tf_op jit(solution)/shard_map/ppermute | solution.py:20
  335.5 2.1 bitcast_dynamic-update-slice_fusion.1
  337.7 34.1 %conditional.7 = (bf16[1,128,1600]{1,2,0:T(8,128)(2,1)}, bf16[1,1,128,768]{3,2,0,1:T(8,128)(2,1)}, bf16[1,1,128,1600]{2,3,0,1:T(8,128)(2,1)}) conditional(s32[]{:T(128)} %convert_element_type.434, () %tuple.72, (s32[]{:T(128)}, bf16[2,1,128,2,128]{4,2,3,0,1:T(8,128)(2,1)}, f32[2,1,2,128,128]{3,4,2,0,1:T(8,128)S(1)}, f32[1,1600]{1,0:T(1,128)S(1)}, ...), branch_computations={%region_11.12_spmd, %region_12.13_spmd} | conditional | flops 454803200 | bytes 11565162 | solution.py:133
  373.8 4.1 all-to-all-start.2
  377.9 2.3 copy.245
  380.3 2.3 copy.259
  382.6 2.4 copy.273
  399.1 16.0 %all-gather.3 = bf16[128,1600]{1,0:T(8,128)(2,1)} all-gather(bf16[16,1600]{1,0:T(8,128)(2,1)S(1)} %convert_element_type.437), channel_id=5, replica_groups=mesh['pipe'=4,'dp'=16,'tensor'=8] {'tensor'}, dimensions={0}, use_global_device_ids=true | all-gather | bytes 460800 | tf_op jit(solution)/shard_map/all_gather | solution.py:139
  425.6 38.5 %collective-permute-done.2 = bf16[1,128,1600]{1,2,0:T(8,128)(2,1)S(1)} collective-permute-done((bf16[1,128,1600]{1,2,0:T(8,128)(2,1)S(1)}, bf16[1,128,1600]{1,2,0:T(8,128)(2,1)S(1)}, u32[]{:S(2)}, u32[]{:S(2)}) %collective-permute-start.2) | collective-permute-done | bytes 409632 | tf_op jit(solution)/shard_map/ppermute | solution.py:20
  465.1 34.2 %conditional.8 = (bf16[1,128,1600]{1,2,0:T(8,128)(2,1)}, bf16[1,1,128,768]{3,2,0,1:T(8,128)(2,1)}, bf16[1,1,128,1600]{2,3,0,1:T(8,128)(2,1)}) conditional(s32[]{:T(128)} %convert_element_type.442, () %tuple.74, (s32[]{:T(128)}, bf16[2,1,128,2,128]{4,2,3,0,1:T(8,128)(2,1)}, f32[2,1,2,128,128]{3,4,2,0,1:T(8,128)S(1)}, f32[1,1600]{1,0:T(1,128)S(1)}, ...), branch_computations={%region_15.16_spmd, %region_16.17_spmd} | conditional | flops 454803200 | bytes 11565162 | solution.py:133
  501.3 4.1 all-to-all-start.3
  524.3 16.0 %all-gather.4 = bf16[128,1600]{1,0:T(8,128)(2,1)} all-gather(bf16[16,1600]{1,0:T(8,128)(2,1)S(1)} %convert_element_type.445), channel_id=6, replica_groups=mesh['pipe'=4,'dp'=16,'tensor'=8] {'tensor'}, dimensions={0}, use_global_device_ids=true | all-gather | bytes 460800 | tf_op jit(solution)/shard_map/all_gather | solution.py:139
  543.9 2.2 fusion.127
  546.1 2.1 collective-permute-start.3
  553.3 36.9 %collective-permute-done.3 = bf16[1,128,1600]{1,2,0:T(8,128)(2,1)} collective-permute-done((bf16[1,128,1600]{1,2,0:T(8,128)(2,1)}, bf16[1,128,1600]{1,2,0:T(8,128)(2,1)}, u32[]{:S(2)}, u32[]{:S(2)}) %collective-permute-start.3) | collective-permute-done | bytes 409632 | tf_op jit(solution)/shard_map/ppermute | solution.py:20
  590.2 2.2 bitcast_dynamic-update-slice_fusion.3
  592.4 2.3 conditional.9
  594.7 2.0 copy.269
  596.7 4.1 all-to-all-start.4
  608.2 76.2 %fusion = bf16[112,1024]{1,0:T(8,128)(2,1)} fusion(bf16[1600,1024]{1,0:T(8,128)(2,1)S(1)} %pad_maximum_fusion.5), kind=kCustom, calls=%all-reduce-scatter | all-reduce-scatter fusion | flops 1835009 | bytes 3508224
  685.4 3.7 collective-permute-start.4
  689.1 4.1 collective-permute-start.5
  693.2 2.0 fusion.112
  703.2 15.6 %all-gather.5 = bf16[128,1600]{1,0:T(8,128)(2,1)S(1)} all-gather(bf16[16,1600]{1,0:T(8,128)(2,1)S(1)} %get-tuple-element.432), channel_id=7, replica_groups=mesh['pipe'=4,'dp'=16,'tensor'=8] {'tensor'}, dimensions={0}, use_global_device_ids=true | all-gather | bytes 460800 | tf_op jit(solution)/shard_map/all_gather | solution.py:139
  721.0 28.9 %all-reduce.3 = (f32[1600]{0:T(1024)S(1)}, f32[1600]{0:T(1024)S(1)}) all-reduce(f32[1600]{0:T(1024)S(1)} %select_add_fusion, f32[1600]{0:T(1024)S(1)} %fusion.112), channel_id=1, replica_groups=mesh['pipe'=4,'dp'=16,'tensor'=8] {'tensor'}, use_global_device_ids=true, to_apply=%region_32.33 | all-reduce | flops 3200 | bytes 25600 | tf_op jit(solution)/shard_map/psum | solution.py:176
  749.9 71.7 %all-reduce.2 = (f32[1,1600]{1,0:T(1,128)S(1)}, f32[1,1600]{1,0:T(1,128)S(1)}) all-reduce(f32[1,1600]{1,0:T(1,128)S(1)} %stack.10, f32[1,1600]{1,0:T(1,128)S(1)} %stack.9), channel_id=1, replica_groups=mesh['pipe'=4,'dp'=16,'tensor'=8] {'dp'}, use_global_device_ids=true, to_apply=%region_33.34 | all-reduce | flops 3200 | bytes 25600 | tf_op jit(solution)/shard_map/psum | solution.py:176
  (232 shorter events, 185.1 us)
Async XLA Ops:
  7.2 20.1 %copy-start.2 = (bf16[2,1,128,1600]{2,3,1,0:T(8,128)(2,1)S(1)}, bf16[2,1,128,1600]{2,3,1,0:T(8,128)(2,1)}, u32[]{:S(2)}) copy-start(bf16[2,1,128,1600]{2,3,1,0:T(8,128)(2,1)} %param.18) | copy-start | bytes 2457604
  7.2 71.6 %all-gather.9.cloned.1.call-start = ((), (), s32[]{:S(2)}) async-start(), calls=%async_computation.5 | async-start | bytes 3620864 | tf_op jit(solution)/shard_map/all_gather | solution.py:51
  27.0 1.1 copy-start.5
  27.3 54.4 %copy-start.44 = (f32[2,128]{1,0:T(2,128)}, f32[2,128]{1,0:T(2,128)S(1)}, u32[]{:S(2)}) copy-start(f32[2,128]{1,0:T(2,128)S(1)} %add_rsqrt_fusion) | copy-start | bytes 3076
  81.7 3.5 copy-start.1
  88.3 0.8 copy-start.35
  88.3 5.4 copy-start.34
  93.7 4.5 copy-start.42
  102.5 18.2 %all-to-all-start = ((bf16[1,8,16,1600]{3,2,0,1:T(8,128)(2,1)}), bf16[1,8,16,1600]{3,2,0,1:T(8,128)(2,1)}, u32[]{:S(2)}, u32[]{:S(2)}) async-start(bf16[1,8,16,1600]{3,2,0,1:T(8,128)(2,1)} %bitcast.535), calls=%async_computation | async-start | bytes 851968 | tf_op jit(solution)/shard_map/all_to_all | solution.py:137
  108.6 2.7 copy-start
  139.9 1.6 copy-start.11
  143.8 43.1 %collective-permute-start = (bf16[1,128,1600]{1,2,0:T(8,128)(2,1)}, bf16[1,128,1600]{1,2,0:T(8,128)(2,1)}, u32[]{:S(2)}, u32[]{:S(2)}) collective-permute-start(bf16[1,128,1600]{1,2,0:T(8,128)(2,1)} %fusion.145), channel_id=1, source_target_pairs={{128,0},{256,128},{384,256},{129,1},{257,129},{385,257},{130,2},{2... | collective-permute-start | bytes 1228808 | tf_op jit(solution)/shard_map/ppermute | solution.py:20
  145.9 41.0 %copy-start.3 = (bf16[2,1,128,1600]{2,3,1,0:T(8,128)(2,1)S(1)}, bf16[2,1,128,1600]{2,3,1,0:T(8,128)(2,1)}, u32[]{:S(2)}) copy-start(bf16[2,1,128,1600]{2,3,1,0:T(8,128)(2,1)} %param.18) | copy-start | bytes 2457604
  188.8 1.1 copy-start.25
  194.6 17.4 %all-to-all-start.1 = ((bf16[1,8,16,1600]{3,2,0,1:T(8,128)(2,1)}), bf16[1,8,16,1600]{3,2,0,1:T(8,128)(2,1)}, u32[]{:S(2)}, u32[]{:S(2)}) async-start(bf16[1,8,16,1600]{3,2,0,1:T(8,128)(2,1)} %bitcast.537), calls=%async_computation.1 | async-start | bytes 851968 | tf_op jit(solution)/shard_map/all_to_all | solution.py:137
  231.2 1.6 copy-start.9
  235.1 100.4 %collective-permute-start.1 = (bf16[1,128,1600]{1,2,0:T(8,128)(2,1)}, bf16[1,128,1600]{1,2,0:T(8,128)(2,1)}, u32[]{:S(2)}, u32[]{:S(2)}) collective-permute-start(bf16[1,128,1600]{1,2,0:T(8,128)(2,1)} %fusion.139), channel_id=1, source_target_pairs={{128,0},{256,128},{384,256},{129,1},{257,129},{385,257},{130,2},{2... | collective-permute-start | bytes 1228808 | tf_op jit(solution)/shard_map/ppermute | solution.py:20
  364.7 1.6 copy-start.20
  373.8 23.6 %all-to-all-start.2 = ((bf16[1,8,16,1600]{3,2,0,1:T(8,128)(2,1)}), bf16[1,8,16,1600]{3,2,0,1:T(8,128)(2,1)}, u32[]{:S(2)}, u32[]{:S(2)}) async-start(bf16[1,8,16,1600]{3,2,0,1:T(8,128)(2,1)} %bitcast.534), calls=%async_computation.2 | async-start | bytes 851968 | tf_op jit(solution)/shard_map/all_to_all | solution.py:137
  398.4 0.7 copy-start.30
  417.0 1.6 copy-start.8
  417.0 5.1 copy-start.41
  418.6 45.4 %copy-start.4 = (bf16[2,1,128,1600]{2,3,1,0:T(8,128)(2,1)S(1)}, bf16[2,1,128,1600]{2,3,1,0:T(8,128)(2,1)}, u32[]{:S(2)}) copy-start(bf16[2,1,128,1600]{2,3,1,0:T(8,128)(2,1)} %param.18) | copy-start | bytes 2457604
  420.1 45.0 %copy-start.22 = (bf16[1,128,1600]{1,2,0:T(8,128)(2,1)}, bf16[1,128,1600]{1,2,0:T(8,128)(2,1)S(1)}, u32[]{:S(2)}) copy-start(bf16[1,128,1600]{1,2,0:T(8,128)(2,1)S(1)} %fusion.133) | copy-start | bytes 1228804
  420.1 43.9 %collective-permute-start.2 = (bf16[1,128,1600]{1,2,0:T(8,128)(2,1)S(1)}, bf16[1,128,1600]{1,2,0:T(8,128)(2,1)S(1)}, u32[]{:S(2)}, u32[]{:S(2)}) collective-permute-start(bf16[1,128,1600]{1,2,0:T(8,128)(2,1)S(1)} %fusion.133), channel_id=1, source_target_pairs={{128,0},{256,128},{384,256},{129,1},{257,129},{385,257},{130,2},{2... | collective-permute-start | bytes 1228808 | tf_op jit(solution)/shard_map/ppermute | solution.py:20
  422.1 43.0 %copy-start.36 = (bf16[3,1,16,1600]{3,2,0,1:T(8,128)(2,1)}, bf16[3,1,16,1600]{3,2,0,1:T(8,128)(2,1)S(1)}, u32[]{:S(2)}) copy-start(bf16[3,1,16,1600]{3,2,0,1:T(8,128)(2,1)S(1)} %constant_dynamic-update-slice_fusion.14) | copy-start | bytes 460804
  492.2 1.6 copy-start.21
  501.3 21.3 %all-to-all-start.3 = ((bf16[1,8,16,1600]{3,2,0,1:T(8,128)(2,1)}), bf16[1,8,16,1600]{3,2,0,1:T(8,128)(2,1)}, u32[]{:S(2)}, u32[]{:S(2)}) async-start(bf16[1,8,16,1600]{3,2,0,1:T(8,128)(2,1)} %bitcast.536), calls=%async_computation.3 | async-start | bytes 851968 | tf_op jit(solution)/shard_map/all_to_all | solution.py:137
  542.3 1.6 copy-start.7
  546.1 44.2 %collective-permute-start.3 = (bf16[1,128,1600]{1,2,0:T(8,128)(2,1)}, bf16[1,128,1600]{1,2,0:T(8,128)(2,1)}, u32[]{:S(2)}, u32[]{:S(2)}) collective-permute-start(bf16[1,128,1600]{1,2,0:T(8,128)(2,1)} %fusion.127), channel_id=1, source_target_pairs={{128,0},{256,128},{384,256},{129,1},{257,129},{385,257},{130,2},{2... | collective-permute-start | bytes 1228808 | tf_op jit(solution)/shard_map/ppermute | solution.py:20
  594.7 7.8 copy-start.6
  594.7 7.8 copy-start.45
  596.7 103.9 %all-to-all-start.4 = ((bf16[1,8,16,1600]{3,2,0,1:T(8,128)(2,1)}), bf16[1,8,16,1600]{3,2,0,1:T(8,128)(2,1)}, u32[]{:S(2)}, u32[]{:S(2)}) async-start(bf16[1,8,16,1600]{3,2,0,1:T(8,128)(2,1)} %bitcast.151), calls=%async_computation.4 | async-start | bytes 851968 | tf_op jit(solution)/shard_map/all_to_all | solution.py:137
  602.5 3.8 copy-start.12
  684.4 11.5 %copy-start.24 = (bf16[112,1024]{1,0:T(8,128)(2,1)S(1)}, bf16[112,1024]{1,0:T(8,128)(2,1)}, u32[]{:S(2)}) copy-start(bf16[112,1024]{1,0:T(8,128)(2,1)} %fusion) | copy-start | bytes 688132
  685.4 10.5 %collective-permute-start.4 = (bf16[112,1024]{1,0:T(8,128)(2,1)}, bf16[112,1024]{1,0:T(8,128)(2,1)S(1)}, u32[]{:S(2)}, u32[]{:S(2)}) collective-permute-start(bf16[112,1024]{1,0:T(8,128)(2,1)} %fusion), channel_id=1, source_target_pairs={{0,8},{8,16},{16,24},{24,32},{32,40},{40,48},{48,56},{56,64},{64,7... | collective-permute-start | bytes 688136
  689.1 6.8 collective-permute-start.5
  693.2 3.4 copy-start.23
  693.2 3.4 copy-start.38
  693.2 3.4 copy-start.39
  697.1 4.7 copy-start.27
  697.1 4.7 copy-start.29
  697.1 4.7 copy-start.31
  697.1 4.7 copy-start.33
  700.6 18.5 %copy-start.10 = (f32[1,1,128,1600]{2,3,1,0:T(8,128)S(1)}, f32[1,1,128,1600]{2,3,1,0:T(8,128)}, u32[]{:S(2)}) copy-start(f32[1,1,128,1600]{2,3,1,0:T(8,128)} %copy.273) | copy-start | bytes 2457604
  703.2 16.3 %copy-start.17 = (bf16[1,128,1600]{1,2,0:T(8,128)(2,1)S(1)}, bf16[1,128,1600]{1,2,0:T(8,128)(2,1)}, u32[]{:S(2)}) copy-start(bf16[1,128,1600]{1,2,0:T(8,128)(2,1)} %get-tuple-element.410) | copy-start | bytes 1228804
  703.2 16.3 %copy-start.46 = (f32[16]{0:T(128)S(1)}, f32[16]{0:T(128)}, u32[]{:S(2)}) copy-start(f32[16]{0:T(128)} %dynamic-slice.8) | copy-start | bytes 196
  719.4 0.9 copy-start.37
  (3 other events, 1.9 us)
Sparse Core Ops, SparseCore 0:
  11.6 67.1 all-gather.8
